TPU v7x, 32 devices: a whole 2x2x4 slice. The times are simulated.
32 devices in a mesh: groups: 2 (over y), out: 8 (over z, x), inp: 2 (over core).
Axes of the slice: x: 2, y: 2, z: 4, core: 2. Of those that a mesh axis runs over, the one named last changes fastest.
Arguments:
- attn: bfloat16 [32, 16384], P(('groups', 'out'), 'inp'), parts along dimension 0, may hold values from -6 to 6
- residual: bfloat16 [32, 16384], P(('groups', 'inp'), 'out'), parts along dimension 0, as said below
- out_weight: bfloat16 [16384, 16384], P('inp', 'out'), as said below
- norm_gain: bfloat16 [16384], P('out'), may hold values from 0.099609375 to 1.8984375
- query_weight: bfloat16 [16384, 16384], P('inp', 'out'), may hold values from -0.046875 to 0.046875
Outputs:
- stream: bfloat16 [32, 16384], P(('groups', 'inp'), 'out'), parts along dimension 0
- queries: bfloat16 [32, 16384], P(('groups', 'inp'), 'out'), parts along dimension 0
There are 2 independent parts, one for each index of `groups`. A program takes and returns all parts, laid end to end along the dimension named above; an argument that names none is the same for every part. Nothing has to cross between parts.
Inputs may be any that keep to these rules, and one draw needn't show every extreme that they name: `residual`: its columns carry scales that differ widely. `out_weight`: entries of the output projection; columns carry scales that differ widely.
All inputs are finite; a program needn't handle non-finite values.
Results may differ from a plain program's by a relative error of at most 0.0057.
Values may be sent and summed in bfloat16 or wider, within the bound.
A program may use at most 192 MiB of HBM per device.

v0:
```python
import jax
import jax.numpy as jnp
from jax import lax
from jax.sharding import PartitionSpec as P

epsilon = 1e-05


def on_device(attn, residual, out_weight, norm_gain, query_weight):
    partial_out = jnp.dot(
        lax.all_gather(attn, "out", axis=0, tiled=True),
        out_weight,
        preferred_element_type=jnp.float32,
    )
    summed = lax.psum_scatter(partial_out, "inp", scatter_dimension=0, tiled=True)
    stream = (residual.astype(jnp.float32) + summed).astype(jnp.bfloat16)
    full_width = norm_gain.shape[0] * lax.axis_size("out")
    values = stream.astype(jnp.float32)
    squares_row = jnp.sum(values * values, axis=1)
    row_total = lax.psum(squares_row, "out")
    factor = lax.rsqrt(row_total / full_width + epsilon)
    normed = (values * factor[:, None] * norm_gain.astype(jnp.float32)[None, :]).astype(
        jnp.bfloat16
    )
    full_rows = lax.all_gather(normed, "out", axis=1, tiled=True)
    feature_half = lax.all_to_all(full_rows, "inp", split_axis=1, concat_axis=0, tiled=True)
    partial_query = jnp.dot(feature_half, query_weight, preferred_element_type=jnp.float32)
    queries = lax.psum_scatter(partial_query, "inp", scatter_dimension=0, tiled=True).astype(
        jnp.bfloat16
    )
    return (stream, queries)


def solution(mesh):
    return jax.shard_map(
        on_device,
        mesh=mesh,
        in_specs=(
            P(("groups", "out"), "inp"),
            P(("groups", "inp"), "out"),
            P("inp", "out"),
            P("out"),
            P("inp", "out"),
        ),
        out_specs=(P(("groups", "inp"), "out"), P(("groups", "inp"), "out")),
        check_vma=False,
    )
```

profile of v0, /device:TPU:0, one launch (start us, length us, event | category | flops | bytes accessed | tf_op | source)
XLA Modules:
  0.0 146.5 jit_solution(1057490435263167405)
XLA Ops:
  7.2 0.0 copy-start.2
  7.2 0.0 copy-start.1
  7.2 0.0 reduce-scatter.3.cloned.1.call-start
  7.2 32.7 %all-gather = bf16[8,2,8192]{2,1,0:T(2,128)(2,1)S(1)} all-gather(bf16[1,2,8192]{2,1,0:T(2,128)(2,1)} %bitcast.11), channel_id=1, replica_groups=mesh['groups'=2,'out'=8,'inp'=2] {'out'}, dimensions={0}, use_global_device_ids=true | all-gather | bytes 294912 | tf_op jit(solution)/shard_map/all_gather | solution.py:11
  40.0 0.1 reshape.10
  40.1 13.5 %fusion.5 = f32[16,2048]{1,0:T(8,128)} fusion(bf16[16,8192]{1,0:T(8,128)(2,1)S(1)} %reshape.10, bf16[8192,2048]{1,0:T(8,128)(2,1)} %param.7), kind=kOutput, calls=%fused_computation.9 | convolution fusion | flops 536870912 | bytes 33947648 | tf_op jit(solution)/shard_map/dot_general | solution.py:10
  53.5 0.0 reduce-scatter.3.cloned.1.call-update
  53.6 0.0 reduce-scatter.5.cloned.1.call-start
  53.6 0.0 copy-done.2
  53.6 8.6 %reduce-scatter.3.cloned.1.call-done = f32[8,2048]{1,0:T(8,128)} async-done(((f32[16,2048]{1,0:T(8,128)}), f32[8,2048]{1,0:T(8,128)}) %reduce-scatter.3.cloned.1.call-update) | async-done | bytes 65552 | tf_op jit(solution)/shard_map/reduce_scatter | solution.py:15
  62.2 0.0 copy-done.1
  62.2 1.0 fusion.2
  63.2 0.0 copy-start
  63.2 21.7 %psum.7 = f32[8]{0:T(128)S(1)} all-reduce(f32[8]{0:T(128)S(1)} %get-tuple-element.2), channel_id=1, replica_groups=mesh['groups'=2,'out'=8,'inp'=2] {'out'}, use_global_device_ids=true, to_apply=%region_2.0 | all-reduce | flops 8 | bytes 64 | tf_op jit(solution)/shard_map/psum | solution.py:20
  84.9 0.1 fusion.4
  85.0 30.9 %all_gather.7 = bf16[8,16384]{1,0:T(8,128)(2,1)S(1)} all-gather(bf16[8,2048]{1,0:T(8,128)(2,1)S(1)} %fusion.4), channel_id=1, replica_groups=mesh['groups'=2,'out'=8,'inp'=2] {'out'}, dimensions={1}, use_global_device_ids=true | all-gather | bytes 294912 | tf_op jit(solution)/shard_map/all_gather | solution.py:25
  115.9 3.9 %all_to_all.19 = bf16[8,2,8192]{2,0,1:T(8,128)(2,1)S(1)} all-to-all(bf16[8,2,8192]{2,0,1:T(8,128)(2,1)S(1)} %bitcast.10), channel_id=1, replica_groups=mesh['groups'=2,'out'=8,'inp'=2] {'inp'}, dimensions={1} | all-to-all | bytes 524288 | tf_op jit(solution)/shard_map/all_to_all | solution.py:26
  119.8 13.5 %fusion = f32[16,2048]{1,0:T(8,128)} fusion(bf16[8192,2048]{1,0:T(8,128)(2,1)} %param.9, bf16[8,2,8192]{2,0,1:T(8,128)(2,1)S(1)} %all_to_all.19), kind=kOutput, calls=%fused_computation | convolution fusion | flops 536870912 | bytes 33947648 | tf_op jit(solution)/shard_map/dot_general | solution.py:27
  133.2 0.0 reduce-scatter.5.cloned.1.call-update
  133.3 4.9 %reduce-scatter.5.cloned.1.call-done = f32[8,2048]{1,0:T(8,128)} async-done(((f32[16,2048]{1,0:T(8,128)}), f32[8,2048]{1,0:T(8,128)}) %reduce-scatter.5.cloned.1.call-update) | async-done | bytes 65552 | tf_op jit(solution)/shard_map/reduce_scatter | solution.py:28
  138.2 1.5 convert_element_type.23
  139.6 0.0 copy-done
  (2 shorter events, 0.0 us)
Async XLA Ops:
  7.2 46.5 %copy-start.2 = (bf16[2048]{0:T(1024)(128)(2,1)S(1)}, bf16[2048]{0:T(1024)(128)(2,1)}, u32[]{:S(2)}) copy-start(bf16[2048]{0:T(1024)(128)(2,1)} %param.8) | copy-start | bytes 12292
  7.2 55.0 %copy-start.1 = (bf16[8,2048]{1,0:T(8,128)(2,1)S(1)}, bf16[8,2048]{1,0:T(8,128)(2,1)}, u32[]{:S(2)}) copy-start(bf16[8,2048]{1,0:T(8,128)(2,1)} %param.6) | copy-start | bytes 98308
  7.2 55.0 %reduce-scatter.3.cloned.1.call-start = ((), (), s32[]{:S(2)}) async-start(), calls=%async_computation.3 | async-start | bytes 196608 | tf_op jit(solution)/shard_map/reduce_scatter | solution.py:15
  53.6 84.6 %reduce-scatter.5.cloned.1.call-start = ((), (), s32[]{:S(2)}) async-start(), calls=%async_computation.4 | async-start | bytes 196608 | tf_op jit(solution)/shard_map/reduce_scatter | solution.py:28
  63.2 76.4 %copy-start = (bf16[8,2048]{1,0:T(8,128)(2,1)}, bf16[8,2048]{1,0:T(8,128)(2,1)S(1)}, u32[]{:S(2)}) copy-start(bf16[8,2048]{1,0:T(8,128)(2,1)S(1)} %get-tuple-element.3) | copy-start | bytes 98308
Sparse Core Ops, SparseCore 0:
  53.7 8.4 reduce-scatter.2
  133.4 4.7 reduce-scatter.4
where the time goes:
time: 147 us; the launch traced here: 146 us
  blocking collectives  89.2 us (61%)
  matrix products  26.9 us (18%)
  between operations  14.1 us (10%)
  waiting for transfers between devices  13.5 us (9%)
  other arithmetic  2.52 us (2%)
    all_gather x1, blocking collectives, on_device(): lax.all_gather(attn, 'out', axis=0, tiled=True)  32.7 us
    all_gather x1, blocking collectives, on_device(): full_rows = lax.all_gather(normed, 'out', axis=1, tiled=True)  30.9 us
    psum x1, blocking collectives, on_device(): row_total = lax.psum(squares_row, 'out')  21.7 us
    dot_general x1, matrix products, on_device(): jnp.dot(lax.all_gather(attn, 'out', axis=0, tiled=True), out_weight, pref...  13.5 us
    dot_general x1, matrix products, on_device(): jnp.dot(feature_half, query_weight, preferred_element_type=jnp.float32)  13.5 us
    reduce_scatter x1, waiting for transfers between devices, on_device(): lax.psum_scatter(partial_out, 'inp', scatter_dimension=0, tiled=True)  8.57 us
    reduce_scatter x1, waiting for transfers between devices, on_device(): lax.psum_scatter(partial_query, 'inp', scatter_dimension=0, tiled=True)  4.89 us
    all_to_all x1, blocking collectives, on_device(): lax.all_to_all(full_rows, 'inp', split_axis=1, concat_axis=0, tiled=True)  3.93 us
  transfers between devices with their start and end apart: 2, of which 2 were waited for; matrix products, arithmetic and copies ran while one was open for 0% of the time, Pallas kernels for 0%

commit v1 on v0

v1 whole, which is shorter than its diff:
```python
import functools

import jax
import jax.numpy as jnp
from jax import lax
from jax.experimental import pallas as pl
from jax.experimental.pallas import tpu as pltpu
from jax.sharding import PartitionSpec as P

epsilon = 1e-05
largest = 1e25
MESH = pl.DeviceIdType.MESH
f32, bf16 = jnp.float32, jnp.bfloat16


def wait_for(ref, sem):
    pltpu.make_async_copy(ref, ref, sem).wait()


def kernel(
    outs, attn, residual_hbm, gain_hbm, w1, w2, stream_o, query_o,
    residual, gain, land, lhs1, w1buf, w2buf, swap_send, swap_recv,
    gbuf, lhs2, ss_part, ss_land, acc, q_recv,
    small_sem, land_send, land_sem, w1_sem, w2_sem, swap_ssem, swap_rsem,
    g_send, g_recv, ss_send, ss_recv, q_ssem, q_rsem,
):
    o, i = lax.axis_index("out"), lax.axis_index("inp")
    half = outs // 2
    blocks, depth, width = w1buf.shape
    slots = w2buf.shape[0]
    rows = lhs1.shape[0]
    mine = rows // 2
    tiles, _, tile = acc.shape
    own = pl.ds(pl.multiple_of(i * mine, 8), mine)
    other = pl.ds(pl.multiple_of((1 - i) * mine, 8), mine)
    home = lax.div(o, half)
    place = lax.rem(o, half)

    barrier = pltpu.get_barrier_semaphore()
    me = o * 2 + i

    def greet(d, c):
        peer = lax.rem(me + d, 2 * outs)
        pl.semaphore_signal(
            barrier, inc=1,
            device_id={"out": lax.div(peer, 2), "inp": lax.rem(peer, 2)},
            device_id_type=MESH,
        )
        return c

    lax.fori_loop(1, 2 * outs, greet, 0)

    pltpu.make_async_copy(attn, land.at[o], land_sem.at[o]).start()
    pltpu.make_async_copy(residual_hbm, residual, small_sem.at[0]).start()
    pltpu.make_async_copy(gain_hbm, gain, small_sem.at[1]).start()

    def w1_copy(j):
        return pltpu.make_async_copy(
            w1.at[:, pl.ds(pl.multiple_of(j * width, 128), width)], w1buf.at[j], w1_sem.at[j]
        )

    full = half * width
    stride = blocks * width

    def w2_start(j):
        slot = lax.rem(j, slots)

        def piece(s, c):
            pltpu.make_async_copy(
                w2.at[pl.ds(pl.multiple_of(s * stride + j * width, 128), width)],
                w2buf.at[slot, pl.ds(pl.multiple_of(s * width, 128), width)],
                w2_sem.at[j, s],
            ).start()
            return c

        lax.fori_loop(0, half, piece, 0)

    for j in range(blocks):
        w1_copy(j).start()

    pl.semaphore_wait(barrier, 2 * outs - 1)

    def attn_copy(d):
        peer = lax.rem(o + d, outs)
        return pltpu.make_async_remote_copy(
            src_ref=attn, dst_ref=land.at[o], send_sem=land_send.at[d], recv_sem=land_sem.at[o],
            device_id={"out": peer}, device_id_type=MESH,
        )

    def loop(first, last, body):
        def step(d, c):
            body(d)
            return c

        lax.fori_loop(first, last, step, 0)

    loop(1, outs, lambda d: attn_copy(d).start())
    for j in range(slots):
        w2_start(j)

    each = land.shape[1]
    batch = 16 // each
    cut = min(1024, depth)

    def assemble(b):
        for t in range(batch):
            wait_for(land.at[b * batch + t], land_sem.at[b * batch + t])

        def columns(c):
            where = pl.ds(pl.multiple_of(c * cut, 128), cut)
            parts = [land[b * batch + t, :, where].astype(f32) for t in range(batch)]
            lhs1[pl.ds(pl.multiple_of(b * 16, 16), 16), where] = jnp.concatenate(
                parts, axis=0
            ).astype(bf16)

        loop(0, depth // cut, columns)

    loop(0, rows // 16, assemble)
    wait_for(residual, small_sem.at[0])
    wait_for(gain, small_sem.at[1])
    ss_part[...] = jnp.zeros_like(ss_part)

    def swap_copy(j):
        return pltpu.make_async_remote_copy(
            src_ref=swap_send.at[j], dst_ref=swap_recv.at[j],
            send_sem=swap_ssem.at[j], recv_sem=swap_rsem.at[j],
            device_id={"inp": 1 - i}, device_id_type=MESH,
        )

    def g_copy(j, t):
        peer = 2 * lax.rem(t + lax.div(o, 2), half) + i
        return pltpu.make_async_remote_copy(
            src_ref=gbuf.at[j],
            dst_ref=lhs2.at[j, :, pl.ds(pl.multiple_of(place * width, 128), width)],
            send_sem=g_send.at[j, t], recv_sem=g_recv.at[j, place],
            device_id={"out": peer, "inp": home}, device_id_type=MESH,
        )

    def g_local(j):
        return pltpu.make_async_copy(
            gbuf.at[j],
            lhs2.at[j, :, pl.ds(pl.multiple_of(place * width, 128), width)],
            g_recv.at[j, place],
        )

    def is_self(t):
        peer = 2 * lax.rem(t + lax.div(o, 2), half) + i
        return jnp.logical_and(peer == o, home == i)

    def post(j):
        where = pl.ds(pl.multiple_of(j * width, 128), width)
        swap_copy(j).wait_recv()
        summed = swap_send[j] + swap_recv[j]
        stream_o[:, where] = (swap_send[j, own, :] + swap_recv[j, own, :]).astype(bf16)
        values = summed.astype(bf16).astype(f32)
        scaled = values * gain[:, where].astype(f32)
        gbuf[j] = jnp.clip(scaled, -largest, largest).astype(bf16)

        def send(t):
            @pl.when(is_self(t))
            def _():
                g_local(j).start()

            @pl.when(jnp.logical_not(is_self(t)))
            def _():
                g_copy(j, t).start()

        loop(0, half, send)
        squares = values * values
        total = ss_part[...]
        for c in range(width // 128):
            total = total + squares[:, c * 128:(c + 1) * 128]
        ss_part[...] = total

    def project(j):
        w1_copy(j).wait()
        swap_send[j] = jnp.dot(lhs1[...], w1buf[j], preferred_element_type=f32)
        where = pl.ds(pl.multiple_of(j * width, 128), width)
        swap_send[j, own, :] += residual[:, where].astype(f32)
        swap_copy(j).start()

        @pl.when(j > 0)
        def _():
            post(j - 1)

    loop(0, blocks, project)
    post(blocks - 1)

    def ss_copy(d):
        peer = lax.rem(o + d, outs)
        return pltpu.make_async_remote_copy(
            src_ref=ss_part.at[own], dst_ref=ss_land.at[o],
            send_sem=ss_send.at[d], recv_sem=ss_recv.at[o],
            device_id={"out": peer}, device_id_type=MESH,
        )

    loop(1, outs, lambda d: ss_copy(d).start())
    ss_land[o] = ss_part[own, :]

    def q_copy(n):
        return pltpu.make_async_remote_copy(
            src_ref=acc.at[n, other], dst_ref=q_recv.at[n],
            send_sem=q_ssem.at[n], recv_sem=q_rsem.at[n],
            device_id={"inp": 1 - i}, device_id_type=MESH,
        )

    def query(j):
        slot = lax.rem(j, slots)

        def arrive(s):
            wait_for(
                lhs2.at[j, :, pl.ds(pl.multiple_of(s * width, 128), width)], g_recv.at[j, s]
            )
            wait_for(
                w2buf.at[slot, pl.ds(pl.multiple_of(s * width, 128), width)], w2_sem.at[j, s]
            )

        loop(0, half, arrive)

        def column(n):
            part = jnp.dot(
                lhs2[j],
                w2buf[slot, :, pl.ds(pl.multiple_of(n * tile, 128), tile)],
                preferred_element_type=f32,
            )

            @pl.when(j == 0)
            def _():
                acc[n] = part

            @pl.when(j > 0)
            def _():
                acc[n] += part

            @pl.when(j == blocks - 1)
            def _():
                q_copy(n).start()

        loop(0, tiles, column)
        if blocks > slots:
            @pl.when(j + slots < blocks)
            def _():
                w2_start(j + slots)

    loop(0, blocks, query)

    def ss_wait(d):
        s = lax.rem(o + d, outs)
        wait_for(ss_land.at[s], ss_recv.at[s])

    loop(1, outs, ss_wait)
    total = lax.fori_loop(
        0, outs, lambda s, t: t + ss_land[s], jnp.zeros((mine, 128), f32)
    )
    mean = jnp.sum(total, axis=1, keepdims=True) / (outs * stride)
    factor = lax.rsqrt(mean + epsilon)
    for n in range(tiles):
        q_copy(n).wait_recv()
        query_o[:, n * tile:(n + 1) * tile] = (
            (acc[n, own, :] + q_recv[n]) * factor
        ).astype(bf16)

    loop(1, outs, lambda d: attn_copy(d).wait_send())
    loop(1, outs, lambda d: ss_copy(d).wait_send())
    for n in range(tiles):
        q_copy(n).wait_send()

    def sent(j):
        swap_copy(j).wait_send()

        def one(t):
            @pl.when(jnp.logical_not(is_self(t)))
            def _():
                g_copy(j, t).wait_send()

        loop(0, half, one)

    loop(0, blocks, sent)


def on_device(outs, attn, residual, out_weight, norm_gain, query_weight):
    each, depth = attn.shape
    mine, features = residual.shape
    rows = 2 * mine
    half = outs // 2
    width = min(512, features)
    blocks = features // width
    slots = min(blocks, 3)
    tile = min(512, features)
    tiles = features // tile
    any_spec = pl.BlockSpec(memory_space=pl.ANY)
    vmem = pl.BlockSpec(memory_space=pltpu.VMEM)
    dma = pltpu.SemaphoreType.DMA
    return pl.pallas_call(
        functools.partial(kernel, outs),
        out_shape=[
            jax.ShapeDtypeStruct((mine, features), bf16),
            jax.ShapeDtypeStruct((mine, features), bf16),
        ],
        in_specs=[any_spec] * 5,
        out_specs=[vmem, vmem],
        scratch_shapes=[
            pltpu.VMEM((mine, features), bf16),
            pltpu.VMEM((1, features), bf16),
            pltpu.VMEM((outs, each, depth), bf16),
            pltpu.VMEM((rows, depth), bf16),
            pltpu.VMEM((blocks, depth, width), bf16),
            pltpu.VMEM((slots, half * width, features), bf16),
            pltpu.VMEM((blocks, rows, width), f32),
            pltpu.VMEM((blocks, rows, width), f32),
            pltpu.VMEM((blocks, rows, width), bf16),
            pltpu.VMEM((blocks, rows, half * width), bf16),
            pltpu.VMEM((rows, 128), f32),
            pltpu.VMEM((outs, mine, 128), f32),
            pltpu.VMEM((tiles, rows, tile), f32),
            pltpu.VMEM((tiles, mine, tile), f32),
            dma((2,)),
            dma((outs,)),
            dma((outs,)),
            dma((blocks,)),
            dma((blocks, half)),
            dma((blocks,)),
            dma((blocks,)),
            dma((blocks, half)),
            dma((blocks, half)),
            dma((outs,)),
            dma((outs,)),
            dma((tiles,)),
            dma((tiles,)),
        ],
        compiler_params=pltpu.CompilerParams(
            collective_id=0, has_side_effects=True, vmem_limit_bytes=62 * 1024 * 1024
        ),
        cost_estimate=pl.CostEstimate(
            flops=4 * rows * depth * features,
            bytes_accessed=4 * depth * features,
            transcendentals=0,
        ),
    )(attn, residual, norm_gain.reshape(1, features), out_weight, query_weight)


def solution(mesh):
    return jax.shard_map(
        functools.partial(on_device, mesh.shape["out"]),
        mesh=mesh,
        in_specs=(
            P(("groups", "out"), "inp"),
            P(("groups", "inp"), "out"),
            P("inp", "out"),
            P("out"),
            P("inp", "out"),
        ),
        out_specs=(P(("groups", "inp"), "out"), P(("groups", "inp"), "out")),
        check_vma=False,
    )
```

time: 147 us -> 34.9 us (0.24)
  blocking collectives: 89.2 us -> 0 us
  Pallas kernels: 0 us -> 30 us
  matrix products: 26.9 us -> 0 us
  waiting for transfers between devices: 13.5 us -> 0 us
  between operations: 14.1 us -> 0.64 us
  local copies, waits for them, and re-layouts: 0.11 us -> 4.04 us
  other arithmetic: 2.52 us -> 0 us
    all_gather x2 -> x0, blocking collectives: 63.6 us -> none  [the longest x1 32.7 us: on_device(): lax.all_gather(attn, 'out', axis=0, tiled=True)]
    pallas_call x0 -> x1, Pallas kernels: none -> 30 us  [on_device(): pl.pallas_call(functools.partial(kernel, outs), out_shape=[jax.ShapeDtype...]
    dot_general x2 -> x0, matrix products: 26.9 us -> none  [the longest x1 13.5 us: on_device(): jnp.dot(lax.all_gather(attn, 'out', axis=0, tiled=True), out_weight, pref...]
    psum x1 -> x0, blocking collectives: 21.7 us -> none  [on_device(): row_total = lax.psum(squares_row, 'out')]
    reduce_scatter x2 -> x0, waiting for transfers between devices: 13.5 us -> none  [the longest x1 8.57 us: on_device(): lax.psum_scatter(partial_out, 'inp', scatter_dimension=0, tiled=True)]
    all_to_all x1 -> x0, blocking collectives: 3.93 us -> none  [on_device(): lax.all_to_all(full_rows, 'inp', split_axis=1, concat_axis=0, tiled=True)]
    unnamed x7 -> x2, local copies, waits for them, and re-layouts: 0.11 us -> 2.75 us
    convert_element_type x3 -> x0, other arithmetic: 1.54 us -> none  [the longest x1 1.46 us: on_device(): lax.psum_scatter(partial_query, 'inp', scatter_dimension=0, tiled=True)]
  transfers between devices with their start and end apart: 2 -> 0, of which waited for: 2 -> 0; matrix products, arithmetic and copies ran while one was open for 0% -> 0% of each run, Pallas kernels for 0% -> 0%
where the time goes in v1:
time: 34.9 us; the launch traced here: 34.6 us
  Pallas kernels  30 us (86%)
  local copies, waits for them, and re-layouts  4.04 us (12%)
  between operations  0.64 us (2%)
    pallas_call x1, Pallas kernels, on_device(): pl.pallas_call(functools.partial(kernel, outs), out_shape=[jax.ShapeDtype...  30 us
    unnamed x2, local copies, waits for them, and re-layouts  2.75 us
    reshape x1, local copies, waits for them, and re-layouts, on_device(): norm_gain.reshape(1, features)  1.29 us

profile of v1, /device:TPU:0, one launch (start us, length us, event | category | flops | bytes accessed | tf_op | source)
XLA Modules:
  0.0 34.6 jit_solution(3934949457204996722)
XLA Ops:
  0.6 1.3 %reshape.7.gain_hbm = bf16[1,2048]{1,0:T(2,128)(2,1)} reshape(bf16[2048]{0:T(1024)(128)(2,1)} %param.8) | data formatting | bytes 8192 | tf_op jit(solution)/shard_map/reshape | solution.py:339
  1.9 30.0 %shard_map.68 = (bf16[8,2048]{1,0:T(8,128)(2,1)}, bf16[8,2048]{1,0:T(8,128)(2,1)}) custom-call(bf16[2,8192]{1,0:T(2,128)(2,1)} %attn.1, bf16[8,2048]{1,0:T(8,128)(2,1)} %residual_hbm.1, bf16[1,2048]{1,0:T(2,128)(2,1)} %reshape.7.gain_hbm, bf16[8192,2048]{1,0:T(8,128)(2,1)} %w1.1, bf16[8192,2048]{1,0:T(8,128)(2,1)} %w2.1), custom_call_target="tpu_custom_call" | custom-call | flops 1073741824 | bytes 67108864 | tf_op jit(solution)/shard_map/pallas_call | solution.py:294
  31.9 1.4 %copy.9 = bf16[8,2048]{1,0:T(8,128)(2,1)} copy(bf16[8,2048]{1,0:T(8,128)(2,1)} %get-tuple-element.4) | data formatting | bytes 65536
  33.3 1.4 %copy.10 = bf16[8,2048]{1,0:T(8,128)(2,1)} copy(bf16[8,2048]{1,0:T(8,128)(2,1)} %get-tuple-element.5) | data formatting | bytes 65536

commit v2 on v1

--- a/solution.py
+++ b/solution.py
@@ -18,8 +18,8 @@
 
 
 def kernel(
-    outs, attn, residual_hbm, gain_hbm, w1, w2, stream_o, query_o,
-    residual, gain, land, lhs1, w1buf, w2buf, swap_send, swap_recv,
+    outs, attn, residual_hbm, gain_hbm, w1, w2, both,
+    residual, gain, gain32, land, lhs1, w1buf, w2buf, swap_send, swap_recv,
     gbuf, lhs2, ss_part, ss_land, acc, q_recv,
     small_sem, land_send, land_sem, w1_sem, w2_sem, swap_ssem, swap_rsem,
     g_send, g_recv, ss_send, ss_recv, q_ssem, q_rsem,
@@ -118,6 +118,7 @@
     loop(0, rows // 16, assemble)
     wait_for(residual, small_sem.at[0])
     wait_for(gain, small_sem.at[1])
+    gain32[...] = gain[...].astype(f32)
     ss_part[...] = jnp.zeros_like(ss_part)
 
     def swap_copy(j):
@@ -151,9 +152,12 @@
         where = pl.ds(pl.multiple_of(j * width, 128), width)
         swap_copy(j).wait_recv()
         summed = swap_send[j] + swap_recv[j]
-        stream_o[:, where] = (swap_send[j, own, :] + swap_recv[j, own, :]).astype(bf16)
+        both[0, :, where] = (swap_send[j, own, :] + swap_recv[j, own, :]).astype(bf16)
         values = summed.astype(bf16).astype(f32)
-        scaled = values * gain[:, where].astype(f32)
+        per = width // 128
+        scaled = values * jnp.concatenate(
+            [gain32[pl.ds(j * per + c, 1), :] for c in range(per)], axis=1
+        )
         gbuf[j] = jnp.clip(scaled, -largest, largest).astype(bf16)
 
         def send(t):
@@ -256,7 +260,7 @@
     factor = lax.rsqrt(mean + epsilon)
     for n in range(tiles):
         q_copy(n).wait_recv()
-        query_o[:, n * tile:(n + 1) * tile] = (
+        both[1, :, n * tile:(n + 1) * tile] = (
             (acc[n, own, :] + q_recv[n]) * factor
         ).astype(bf16)
 
@@ -291,17 +295,15 @@
     any_spec = pl.BlockSpec(memory_space=pl.ANY)
     vmem = pl.BlockSpec(memory_space=pltpu.VMEM)
     dma = pltpu.SemaphoreType.DMA
-    return pl.pallas_call(
+    results = pl.pallas_call(
         functools.partial(kernel, outs),
-        out_shape=[
-            jax.ShapeDtypeStruct((mine, features), bf16),
-            jax.ShapeDtypeStruct((mine, features), bf16),
-        ],
+        out_shape=[jax.ShapeDtypeStruct((2, mine, features), bf16)],
         in_specs=[any_spec] * 5,
-        out_specs=[vmem, vmem],
+        out_specs=[vmem],
         scratch_shapes=[
             pltpu.VMEM((mine, features), bf16),
-            pltpu.VMEM((1, features), bf16),
+            pltpu.VMEM((features // 128, 128), bf16),
+            pltpu.VMEM((features // 128, 128), f32),
             pltpu.VMEM((outs, each, depth), bf16),
             pltpu.VMEM((rows, depth), bf16),
             pltpu.VMEM((blocks, depth, width), bf16),
@@ -336,7 +338,8 @@
             bytes_accessed=4 * depth * features,
             transcendentals=0,
         ),
-    )(attn, residual, norm_gain.reshape(1, features), out_weight, query_weight)
+    )(attn, residual, norm_gain.reshape(features // 128, 128), out_weight, query_weight)
+    return results[0][0], results[0][1]
 
 
 def solution(mesh):

time: 34.9 us -> 32.4 us (0.928)
  local copies, waits for them, and re-layouts: 4.04 us -> 1.4 us
    unnamed x2 -> x0, local copies, waits for them, and re-layouts: 2.75 us -> none
    squeeze x0 -> x1, local copies, waits for them, and re-layouts: none -> 1.4 us  [on_device(): return (results[0][0], results[0][1])]
    reshape x1 -> x0, local copies, waits for them, and re-layouts: 1.29 us -> none  [on_device(): norm_gain.reshape(1, features)]
where the time goes in v2:
time: 32.4 us; the launch traced here: 32.2 us
  Pallas kernels  30.2 us (93%)
  local copies, waits for them, and re-layouts  1.4 us (4%)
  between operations  0.64 us (2%)
    pallas_call x1, Pallas kernels, on_device(): pl.pallas_call(functools.partial(kernel, outs), out_shape=[jax.ShapeDtype...  30.2 us
    squeeze x1, local copies, waits for them, and re-layouts, on_device(): return (results[0][0], results[0][1])  1.4 us

profile of v2, /device:TPU:0, one launch (start us, length us, event | category | flops | bytes accessed | tf_op | source)
XLA Modules:
  0.0 32.2 jit_solution(3462141358493388319)
XLA Ops:
  0.6 30.2 %shard_map.68 = bf16[2,8,2048]{2,1,0:T(8,128)(2,1)} custom-call(bf16[2,8192]{1,0:T(2,128)(2,1)} %attn.1, bf16[8,2048]{1,0:T(8,128)(2,1)} %residual_hbm.1, bf16[16,128]{1,0:T(8,128)(2,1)} %bitcast.5, bf16[8192,2048]{1,0:T(8,128)(2,1)} %w1.1, bf16[8192,2048]{1,0:T(8,128)(2,1)} %w2.1), custom_call_target="tpu_custom_call" | custom-call | flops 1073741824 | bytes 67108864 | tf_op jit(solution)/shard_map/pallas_call | solution.py:298
  30.8 1.4 %slice_bitcast_fusion = (bf16[8,2048]{1,0:T(8,128)(2,1)}, bf16[8,2048]{1,0:T(8,128)(2,1)}) fusion(bf16[2,8,2048]{2,1,0:T(8,128)(2,1)} %shard_map.68), kind=kLoop, calls=%fused_computation | loop fusion | bytes 131072 | tf_op jit(solution)/shard_map/squeeze | solution.py:342

commit v3 on v2

--- a/solution.py
+++ b/solution.py
@@ -48,7 +48,7 @@
         )
         return c
 
-    lax.fori_loop(1, 2 * outs, greet, 0)
+    lax.fori_loop(1, 2 * outs, greet, 0, unroll=outs <= 8)
 
     pltpu.make_async_copy(attn, land.at[o], land_sem.at[o]).start()
     pltpu.make_async_copy(residual_hbm, residual, small_sem.at[0]).start()
@@ -59,7 +59,6 @@
             w1.at[:, pl.ds(pl.multiple_of(j * width, 128), width)], w1buf.at[j], w1_sem.at[j]
         )
 
-    full = half * width
     stride = blocks * width
 
     def w2_start(j):
@@ -80,8 +79,13 @@
 
     pl.semaphore_wait(barrier, 2 * outs - 1)
 
+    def peer_of(d):
+        near = lax.div(d - 1, half)
+        block = near * home + (1 - near) * (1 - home)
+        return block * half + lax.rem(place + d, half)
+
     def attn_copy(d):
-        peer = lax.rem(o + d, outs)
+        peer = peer_of(d)
         return pltpu.make_async_remote_copy(
             src_ref=attn, dst_ref=land.at[o], send_sem=land_send.at[d], recv_sem=land_sem.at[o],
             device_id={"out": peer}, device_id_type=MESH,
@@ -128,8 +132,14 @@
             device_id={"inp": 1 - i}, device_id_type=MESH,
         )
 
+    def g_peer(t):
+        quarter = half // 2
+        near = lax.div(t, quarter)
+        block = near * home + (1 - near) * (1 - home)
+        return block * half + 2 * lax.rem(t + lax.div(place, 2), quarter) + i
+
     def g_copy(j, t):
-        peer = 2 * lax.rem(t + lax.div(o, 2), half) + i
+        peer = g_peer(t)
         return pltpu.make_async_remote_copy(
             src_ref=gbuf.at[j],
             dst_ref=lhs2.at[j, :, pl.ds(pl.multiple_of(place * width, 128), width)],
@@ -145,7 +155,7 @@
         )
 
     def is_self(t):
-        peer = 2 * lax.rem(t + lax.div(o, 2), half) + i
+        peer = g_peer(t)
         return jnp.logical_and(peer == o, home == i)
 
     def post(j):

time: 32.4 us -> 31.6 us (0.975)
  Pallas kernels: 30.2 us -> 29.4 us
    pallas_call x1, Pallas kernels: 30.2 us -> 29.4 us  [on_device(): pl.pallas_call(functools.partial(kernel, outs), out_shape=[jax.ShapeDtype...]
where the time goes in v3:
time: 31.6 us; the launch traced here: 31.5 us
  Pallas kernels  29.4 us (93%)
  local copies, waits for them, and re-layouts  1.4 us (4%)
  between operations  0.64 us (2%)
    pallas_call x1, Pallas kernels, on_device(): pl.pallas_call(functools.partial(kernel, outs), out_shape=[jax.ShapeDtype...  29.4 us
    squeeze x1, local copies, waits for them, and re-layouts, on_device(): return (results[0][0], results[0][1])  1.4 us

profile of v3, /device:TPU:0, one launch (start us, length us, event | category | flops | bytes accessed | tf_op | source)
XLA Modules:
  0.0 31.5 jit_solution(1310870612018370788)
XLA Ops:
  0.6 29.4 %shard_map.68 = bf16[2,8,2048]{2,1,0:T(8,128)(2,1)} custom-call(bf16[2,8192]{1,0:T(2,128)(2,1)} %attn.1, bf16[8,2048]{1,0:T(8,128)(2,1)} %residual_hbm.1, bf16[16,128]{1,0:T(8,128)(2,1)} %bitcast.5, bf16[8192,2048]{1,0:T(8,128)(2,1)} %w1.1, bf16[8192,2048]{1,0:T(8,128)(2,1)} %w2.1), custom_call_target="tpu_custom_call" | custom-call | flops 1073741824 | bytes 67108864 | tf_op jit(solution)/shard_map/pallas_call | solution.py:308
  30.1 1.4 %slice_bitcast_fusion = (bf16[8,2048]{1,0:T(8,128)(2,1)}, bf16[8,2048]{1,0:T(8,128)(2,1)}) fusion(bf16[2,8,2048]{2,1,0:T(8,128)(2,1)} %shard_map.68), kind=kLoop, calls=%fused_computation | loop fusion | bytes 131072 | tf_op jit(solution)/shard_map/squeeze | solution.py:352
